TPU v7x, 32 devices: a whole 2x2x4 slice. The times are simulated.
32 devices in a mesh: groups: 2 (over y), rows: 8 (over z, x), member: 2 (over core).
Axes of the slice: x: 2, y: 2, z: 4, core: 2. Of those that a mesh axis runs over, the one named last changes fastest.
Arguments:
- features: bfloat16 [16384, 512], P(('groups', 'rows')), parts along dimension 0, may hold values from -6 to 6
- escalated: int32 [16, 256], P(('groups', 'rows')), parts along dimension 0, may hold values from 0 to 1023, as said below
- owner_ids: int32 [16, 256, 1], P(('groups', 'rows')), parts along dimension 0, may hold values from 0 to 7; in each aligned block of 256 rows (0 to 255, 256 to 511, ..., all dimensions but the last counted through in order) at most 64 rows name the same one
- member_in: bfloat16 [4, 512, 1024], P('member'), may hold values from -0.25 to 0.25
- member_bias: float32 [4, 1024], P('member'), may hold values from -3 to 3
- member_out: bfloat16 [4, 1024], P('member'), may hold values from -0.1875 to 0.1875
- feat_weight: bfloat16 [512, 512], P('member'), may hold values from -0.25 to 0.25
- feat_bias: float32 [512], replicated, may hold values from -5 to 5
- pred_scale: float32 [4, 512], replicated, may hold values from -5 to 5
- pred_shift: float32 [4, 512], replicated, may hold values from -5 to 5
- cls_token: float32 [512], replicated, may hold values from -5 to 5
- attn_gain: float32 [512], replicated, may hold values from 0.1 to 1.9
- qkv_weight: bfloat16 [3, 512, 512], P(None, None, 'member'), may hold values from -0.25 to 0.25
- out_weight: bfloat16 [512, 512], P('member'), may hold values from -0.25 to 0.25
- ffn_gain: float32 [512], replicated, may hold values from 0.1 to 1.9
- up_weight: bfloat16 [8, 512, 1024], P('rows', None, 'member'), may hold values from -0.25 to 0.25
- up_bias: float32 [8, 1024], P('rows', 'member'), may hold values from -3 to 3
- down_weight: bfloat16 [8, 1024, 512], P('rows', 'member'), may hold values from -0.1875 to 0.1875
- owner_heads: float32 [8, 512], P('rows'), may hold values from -0.25 to 0.25
Outputs:
- scores: float32 [16384], P(('groups', 'rows')), parts along dimension 0
There are 2 independent parts, one for each index of `groups`. A program takes and returns all parts, laid end to end along the dimension named above; an argument that names none is the same for every part. Nothing has to cross between parts.
Inputs may be any that keep to these rules, and one draw needn't show every extreme that they name: Each row of escalated lists 256 distinct local row indices of its shard. `owner_ids`: within one row shard at most 64 escalated rows have the same segment.
All inputs are finite; a program needn't handle non-finite values.
Results may differ from a plain program's by a relative error of at most 0.0034.
Values may be sent and summed in bfloat16 or wider, within the bound.
No kernel may reach another device: no remote copies, remote signals or barrier semaphores. Data moves between devices by JAX's collectives and lax.ppermute only.
A program may use at most 64 MiB of HBM per device.

v0:
```python
import functools
import math

import jax
import jax.numpy as jnp
from jax import lax
from jax.experimental import pallas as pl
from jax.experimental.pallas import tpu as pltpu
from jax.sharding import PartitionSpec as P

HD = 64
EPS = 1e-05
LANES = 128
BF = jnp.bfloat16
F32 = jnp.float32
VMEM = pl.BlockSpec(memory_space=pltpu.VMEM)
HBM = pl.BlockSpec(memory_space=pltpu.HBM)
ANY = pl.BlockSpec(memory_space=pl.ANY)
GELU_C = math.sqrt(2.0 / math.pi)

KMAP, VCLS, LCLS, SCALE, SHIFT, GAIN, FBIAS, CLS, FGAIN = 0, 8, 9, 16, 24, 32, 33, 34, 35
TABLE = 40
DOWN, BIAS, HEAD, EXTRA = 0, 3, 6, 16


def iota(shape, dim):
    return lax.broadcasted_iota(jnp.int32, shape, dim)


def gelu2(x):
    return x + x * jnp.tanh(x * (GELU_C + (GELU_C * 0.044715) * (x * x)))


def dot(a, b):
    return lax.dot_general(a, b, (((1,), (0,)), ((), ())), preferred_element_type=F32)


def dot_t(a, b):
    return lax.dot_general(a, b, (((1,), (1,)), ((), ())), preferred_element_type=F32)


def split2(x):
    high = x.astype(BF)
    return high, (x - high.astype(F32)).astype(BF)


def split3(x):
    high, rest = x.astype(BF), x
    rest = rest - high.astype(F32)
    mid = rest.astype(BF)
    low = (rest - mid.astype(F32)).astype(BF)
    return jnp.concatenate([high.astype(F32), mid.astype(F32), low.astype(F32)], axis=0).astype(BF)


def join3(x):
    rows = x.shape[0] // 3
    return x[:rows] + x[rows : 2 * rows] + x[2 * rows :]


def centre(x):
    return x - jnp.mean(x, axis=-1, keepdims=True)


def inverse_spread(centered):
    return lax.rsqrt(jnp.mean(centered * centered, axis=-1, keepdims=True) + EPS)


def start_all(pairs, sems):
    copies = [pltpu.make_async_copy(src, dst, sems.at[i]) for i, (src, dst) in enumerate(pairs)]
    for copy in copies:
        copy.start()
    return copies


def route_kernel(
    n, half, relative, esc_hbm, own_hbm, feat_hbm, w_hbm, bias_hbm, out_hbm, down_hbm, upb_hbm, head_hbm, up_hbm,
    qkv_hbm, fw_hbm, ow_hbm, index_ref, rows_ref, near_ref, far_ref, segment_ref, qkv_ref, both_ref,
    esc_ref, own_ref, feat_ref, w_ref, bias_ref, out_ref, down_ref, upb_ref, head_ref, sems,
):
    depth = up_hbm.shape[1]
    here = w_hbm.shape[0]
    copies = start_all(
        [(esc_hbm, esc_ref), (own_hbm, own_ref), (feat_hbm, feat_ref), (bias_hbm, bias_ref), (out_hbm, out_ref)]
        + [(w_hbm.at[m], w_ref.at[m]) for m in range(here)], sems)
    core = lax.axis_index("member")
    count = esc_hbm.shape[1]
    dealt = count // 2
    copies[0].wait()
    copies[1].wait()
    esc = esc_ref[...]
    own = own_ref[...]
    ii = iota((count, count), 0)
    jj = iota((count, count), 1)
    diag = ii == jj

    def to_col(row):
        return jnp.sum(jnp.where(diag, row, 0).astype(F32), axis=1, keepdims=True)

    own_col = to_col(own).astype(jnp.int32)
    before = jnp.sum((own_col < own).astype(F32), axis=0, keepdims=True).astype(jnp.int32)
    rank = jnp.sum(((own_col == own) & (ii < jj)).astype(F32), axis=0, keepdims=True).astype(jnp.int32)
    position = before + rank
    side = position & 1
    slot = rank >> 1
    me = lax.axis_index("rows")
    apart = own ^ me
    pair = (apart if relative else (own - (own & 1)) + (apart & 1))
    place = pair * half + slot
    dense = (position >> 1) + jnp.where(side == core, 0, dealt)
    mine = dense == ii
    source = jnp.sum(jnp.where(mine, esc, 0).astype(F32), axis=1, keepdims=True).astype(jnp.int32)
    chosen = (source == iota((count, feat_ref.shape[0]), 1)).astype(F32).astype(BF)
    copies[2].wait()
    copies += start_all(
        [(head_hbm, head_ref), (upb_hbm, upb_ref), (down_hbm, down_ref), (fw_hbm, both_ref.at[: fw_hbm.shape[0]]),
         (ow_hbm, both_ref.at[fw_hbm.shape[0] :]),
         (up_hbm.at[0], segment_ref.at[:depth]), (qkv_hbm, qkv_ref)], sems.at[pl.ds(5 + here, 7)])
    rows = dot(chosen, feat_ref[...]).astype(BF)
    rows_ref[...] = rows[:dealt]
    lane = iota((LANES, 1), 0)
    preds = None
    copies[3].wait()
    copies[4].wait()
    for m in range(here):
        copies[5 + m].wait()
        act = gelu2(dot(rows, w_ref[m]) + bias_ref[m : m + 1]).astype(BF)
        on_lane = jnp.where(lane == core * here + m, 0.5 * out_ref[m : m + 1].astype(F32), 0.0).astype(BF)
        pred = dot_t(act, on_lane)
        preds = pred if preds is None else preds + pred
    preds = preds.astype(BF)
    near_ref[...] = preds[:dealt]
    far_ref[...] = preds[dealt:]

    line = pair >> 1
    line = line * (n // 2 + 1) + (side ^ core) * (n // 2) ** 2 if relative else line + (side ^ core) * (n // 2)
    for i, row in enumerate((line, (apart & 1) * half + slot, esc, place, dense)):
        index_ref[i : i + 1, :] = row

    for copy in copies[5 + here : 8 + here]:
        copy.wait()
    head = jnp.broadcast_to(head_ref[...], (8, head_ref.shape[1]))
    down = join3(dot_t(split3(head), down_ref[0]))[0:1]
    extra = [split3(x).astype(F32) for x in (down, upb_ref[...], head_ref[...])]
    extra.append(jnp.zeros((EXTRA - 9, down.shape[1]), F32))
    segment_ref[depth:, :] = jnp.concatenate(extra, axis=0).astype(BF)
    for copy in copies[8 + here :]:
        copy.wait()


def constants_kernel(
    cls_ref, gain_ref, scale_ref, shift_ref, fbias_ref, fgain_ref, q0_ref, q1_ref, index_ref,
    table_ref, where_ref, place_ref,
):
    count = index_ref.shape[1]
    diag = iota((count, count), 0) == iota((count, count), 1)
    cols = [
        jnp.sum(jnp.where(diag, index_ref[i : i + 1, :], 0).astype(F32), axis=1, keepdims=True) for i in range(5)]
    for i in range(3):
        where_ref[:, i : i + 1] = cols[i].astype(jnp.int32)
    dealt = place_ref.shape[1]
    placed = cols[4].astype(jnp.int32) == iota((count, dealt), 1)
    place_ref[...] = jnp.sum(jnp.where(placed, cols[3], 0.0), axis=0, keepdims=True).astype(jnp.int32)
    gain = gain_ref[...]
    cls = cls_ref[...]
    centered = centre(cls)
    ncls = (centered * inverse_spread(centered) * gain).astype(BF)
    table_ref[...] = jnp.zeros_like(table_ref)
    members = scale_ref.shape[0]
    table_ref[SCALE : SCALE + members, :] = centre(scale_ref[...])
    table_ref[SHIFT : SHIFT + members, :] = centre(shift_ref[...])
    table_ref[GAIN : GAIN + 1, :] = gain
    table_ref[FBIAS : FBIAS + 1, :] = fbias_ref[...]
    table_ref[CLS : CLS + 1, :] = cls
    table_ref[FGAIN : FGAIN + 1, :] = fgain_ref[...]
    lhs = jnp.broadcast_to(ncls.astype(F32), (8, ncls.shape[1])).astype(BF)
    local = q0_ref.shape[2]
    heads = local // HD
    row = iota((8, local), 0)
    col = iota((8, local), 1) // HD
    kmap = None
    for i, ref in enumerate((q0_ref, q1_ref)):
        query = dot(lhs, ref[0]) * (1.0 / math.sqrt(HD))
        spread = jnp.where(row == col + i * heads, query, 0.0)
        part = join3(dot_t(split3(spread), ref[1]))
        kmap = part if kmap is None else kmap + part
        table_ref[VCLS : VCLS + 1, i * local : (i + 1) * local] = dot(lhs, ref[2])[0:1]
    table_ref[KMAP : KMAP + 8, :] = kmap
    logits = jnp.sum(kmap * ncls.astype(F32), axis=-1, keepdims=True)
    eye = iota((8, LANES), 0) == iota((8, LANES), 1)
    table_ref[LCLS : LCLS + 1, :LANES] = jnp.sum(jnp.where(eye, logits, 0.0), axis=0, keepdims=True)


def attend_kernel(
    members, rows_ref, near_ref, far_ref, place_ref, table_ref, fw0_ref, fw1_ref, q0_ref, q1_ref, *sent_refs
):
    core = lax.axis_index("member")
    rows = rows_ref[...]
    total, fwidth = rows.shape
    local = q0_ref.shape[2]
    gain = table_ref[GAIN : GAIN + 1, :]
    low, high = rows[:, : fwidth // 2].astype(F32), rows[:, fwidth // 2 :].astype(F32)
    first = jnp.where(core == 0, low, high).astype(BF)
    second = jnp.where(core == 0, high, low).astype(BF)
    token = dot(first, fw0_ref[: fwidth // 2]) + dot(second, fw1_ref[: fwidth // 2]) + table_ref[FBIAS : FBIAS + 1, :]
    centered = centre(token)
    tokens = [(centered * inverse_spread(centered) * gain).astype(BF)]
    preds = near_ref[...].astype(F32) + far_ref[...].astype(F32)
    for m in range(members):
        centered = preds[:, m : m + 1] * table_ref[SCALE + m : SCALE + m + 1, :] + table_ref[SHIFT + m : SHIFT + m + 1, :]
        tokens.append((centered * inverse_spread(centered) * gain).astype(BF))
    normed = jnp.concatenate(tokens, axis=0)
    count = len(tokens)

    kmap = jnp.concatenate([table_ref[KMAP : KMAP + 8, :], jnp.zeros((LANES - 8, table_ref.shape[1]), F32)], axis=0)
    logits = dot_t(normed, jnp.concatenate(split2(kmap), axis=0))
    logits = logits[:, :LANES] + logits[:, LANES:]
    expo = jnp.exp(logits)
    expo_cls = jnp.exp(table_ref[LCLS : LCLS + 1, :LANES])
    norm = expo_cls
    for t in range(count):
        norm = norm + expo[t * total : (t + 1) * total]
    inverse = 1.0 / norm
    weights = jnp.concatenate(
        [expo[t * total : (t + 1) * total] * inverse for t in range(count)] + [expo_cls * inverse], axis=0)
    expand = (iota((2 * LANES, 2 * local), 0) & (LANES - 1)) == iota((2 * LANES, 2 * local), 1) // HD
    spread = dot(jnp.concatenate(split2(weights), axis=1), expand.astype(F32).astype(BF))
    parts = []
    for i, ref in enumerate((q0_ref, q1_ref)):
        at = slice(i * local, (i + 1) * local)
        value = dot(normed, ref[2])
        mixed = spread[count * total :, at] * table_ref[VCLS : VCLS + 1, at]
        for t in range(count):
            rng = slice(t * total, (t + 1) * total)
            mixed = mixed + spread[rng, at] * value[rng]
        parts.append(mixed)
    mixed = jnp.concatenate(parts, axis=1).astype(BF)
    size = sent_refs[0].shape[0]
    scatter = (place_ref[...] == iota((size * len(sent_refs), total), 0)).astype(F32).astype(BF)
    sent = dot(scatter, mixed).astype(BF)
    for k, sent_ref in enumerate(sent_refs):
        sent_ref[...] = sent[k * size : (k + 1) * size]


def ensemble_kernel(first, count, tile, feat_ref, w_ref, bias_ref, out_ref, after_ref, *refs):
    held = (len(refs) - 1) // 2
    copies = start_all(list(zip(refs[:held], refs[held + 1 :])), refs[-1]) if held else []
    pred_ref = refs[held]
    for t in range(count):
        rows = feat_ref[(first + t) * tile : (first + t + 1) * tile]
        total = None
        for m in range(w_ref.shape[0]):
            hidden = gelu2(dot(rows, w_ref[m]) + bias_ref[m : m + 1]).astype(BF)
            weights = jnp.broadcast_to(out_ref[m : m + 1].astype(F32), (8, out_ref.shape[1])).astype(BF)
            pred = dot_t(weights, hidden)[0:1]
            total = pred if total is None else total + pred
        per = tile // LANES
        for i in range(per):
            pred_ref[t * per + i : t * per + i + 1, :] = total[:, i * LANES : (i + 1) * LANES]
    for copy in copies:
        copy.wait()


def unpack(ref):
    depth = ref.shape[0] - EXTRA
    extra = ref[depth:, :].astype(F32)
    return ref[:depth, :], *(jnp.sum(extra[i : i + 3], axis=0, keepdims=True) for i in (DOWN, BIAS, HEAD))


def hidden_terms(normed, up, down, bias):
    return jnp.maximum(dot(normed, up) + bias, 0.0).astype(BF).astype(F32) * down


def states(mixed, table_ref, both0_ref, both1_ref):
    local = mixed.shape[1] // 2
    ow0, ow1 = (ref[ref.shape[0] - local :] for ref in (both0_ref, both1_ref))
    state = table_ref[CLS : CLS + 1, :] + dot(mixed[:, :local], ow0) + dot(mixed[:, local:], ow1)
    centered = centre(state)
    return state, (centered * inverse_spread(centered) * table_ref[FGAIN : FGAIN + 1, :]).astype(BF)


def arrived(got_refs, half, e):
    if len(got_refs) == 1:
        rows = got_refs[0].shape[0] // 2
        return got_refs[0][e * rows : (e + 1) * rows]
    return jnp.concatenate([ref[e * half : (e + 1) * half] for ref in got_refs], axis=0)


def arrive_kernel(blocks, half, *refs):
    table_ref, both0_ref, both1_ref, state_ref, normed_ref = refs[blocks:]
    state_ref[...], normed_ref[...] = states(arrived(refs[:blocks][::-1], half, 1), table_ref, both0_ref, both1_ref)


def near_score_kernel(blocks, half, *refs):
    table_ref, both0_ref, both1_ref, up0_ref, up1_ref, next_hbm, score_ref, next_ref, sems = refs[blocks:]
    (copy,) = start_all([(next_hbm, next_ref)], sems)
    state, normed = states(arrived(refs[:blocks][::-1], half, 0), table_ref, both0_ref, both1_ref)
    up, down, bias, head = unpack(up0_ref)
    terms = state * head + hidden_terms(normed, up, down, bias)
    up, down, bias, _ = unpack(up1_ref)
    terms = terms + hidden_terms(normed, up, down, bias)
    score_ref[...] = jnp.sum(terms, axis=-1, keepdims=True)
    copy.wait()


def far_score_kernel(blocks, half, near_ref, state_ref, mine_ref, other_ref, up2_ref, out_ref):
    rows = near_ref.shape[0]
    up, down, bias, head = unpack(up2_ref)
    terms = hidden_terms(jnp.concatenate([mine_ref[...], other_ref[...]], axis=0), up, down, bias)
    scores = [
        near_ref[...],
        jnp.sum(terms[:rows] + state_ref[...] * head, axis=-1, keepdims=True),
        jnp.sum(terms[rows:], axis=-1, keepdims=True),
    ]
    if blocks == 1:
        eye = iota((rows, rows), 0) == iota((rows, rows), 1)
        for e, score in enumerate(scores):
            out_ref[:, e * rows : (e + 1) * rows] = jnp.sum(jnp.where(eye, score, 0.0), axis=0, keepdims=True)
    else:
        row, lane = iota((half, LANES), 0), iota((half, LANES), 1)
        for k in range(blocks):
            line = jnp.zeros((half, LANES), F32)
            for e, score in enumerate(scores):
                line = jnp.where(lane == row + e * half, score[k * half : (k + 1) * half], line)
            out_ref[k : k + 1, :] = jnp.sum(line, axis=0, keepdims=True)


def expand_kernel(lines, where_ref, after_ref, line_ref, lane_ref):
    rows = lane_ref.shape[1]
    hit = where_ref[:, 2:3] == iota((where_ref.shape[0], rows), 1)

    def by_row(i):
        return jnp.sum(jnp.where(hit, where_ref[:, i : i + 1] + 1, 0).astype(F32), axis=0, keepdims=True).astype(jnp.int32)

    line = (by_row(0) - 1 == iota((lines, rows), 0)).astype(F32)
    line_ref[...] = jnp.concatenate([line] * 3, axis=0).astype(BF)
    lane_ref[...] = by_row(1) - 1


def finish_kernel(members, half, lines, line_ref, lane_ref, near_ref, far_ref, out_ref):
    near, far = near_ref[...], far_ref[...]
    ensemble = (near[lines:] + far[lines:]) * (0.5 / members)
    ensemble = jnp.concatenate([ensemble[i : i + 1] for i in range(ensemble.shape[0])], axis=1)
    lanes = iota((lines, LANES), 1)
    last = (lanes >= half) & (lanes < 2 * half)

    def whole(mine, others):
        return mine[:lines] + jnp.where(last, pltpu.roll(others[:lines], LANES - half, 1), 0.0)

    table = split3(jnp.concatenate([whole(near, far), whole(far, near)], axis=0))
    by_lane = lax.dot_general(table, line_ref[...], (((0,), (0,)), ((), ())), preferred_element_type=F32)
    lane = lane_ref[...]
    replaced = jnp.sum(jnp.where(lane == iota(by_lane.shape, 0), by_lane, 0.0), axis=0, keepdims=True)
    out_ref[...] = jnp.where(lane >= 0, replaced, ensemble)


def cost(flops, size, trans=0):
    return pl.CostEstimate(flops=flops, bytes_accessed=size, transcendentals=trans)


def params(mib):
    return pltpu.CompilerParams(vmem_limit_bytes=mib * 2**20)


def in_hbm(arrays):
    return [pltpu.with_memory_space_constraint(x, pltpu.HBM) for x in arrays]


def shape(dims, dtype):
    return jax.ShapeDtypeStruct(dims, dtype)


def per_device(
    features, escalated, owner_ids, member_in, member_bias, member_out, feat_weight, feat_bias,
    pred_scale, pred_shift, cls_token, attn_gain, qkv_weight, out_weight, ffn_gain, up_weight,
    up_bias, down_weight, owner_heads,
):
    n = lax.axis_size("rows")
    rows, fwidth = features.shape
    count = escalated.shape[1]
    half = max(1, count // n)
    slots = n * half
    here, _, hidden = member_in.shape
    members = pred_scale.shape[0]
    width = cls_token.shape[0]

    def swap(x):
        return lax.ppermute(x, "member", [(0, 1), (1, 0)])

    row = lambda x: x.reshape(1, -1)
    cls_token, attn_gain, ffn_gain, feat_bias = map(row, (cls_token, attn_gain, ffn_gain, feat_bias))
    owners = owner_ids.reshape(1, count)

    pairs = n // 2
    relative = pairs <= 8
    blocks = pairs if relative else 1
    other_qkv = swap(qkv_weight)

    dealt = count // 2
    ins = (escalated, owners, features, member_in, member_bias, member_out, down_weight, up_bias, owner_heads, up_weight,
           qkv_weight, feat_weight, out_weight)
    index, mine, near, far, segment, own_qkv, own_both = pl.pallas_call(
        functools.partial(route_kernel, n, half, relative),
        out_shape=[shape((8, count), jnp.int32), shape((dealt, fwidth), BF), shape((dealt, LANES), BF),
                   shape((dealt, LANES), BF), shape((up_weight.shape[1] + EXTRA, up_weight.shape[2]), BF),
                   shape(qkv_weight.shape, BF), shape((feat_weight.shape[0] + out_weight.shape[0], width), BF)],
        in_specs=[HBM] * len(ins),
        out_specs=[VMEM] * 7,
        scratch_shapes=[pltpu.VMEM(x.shape, x.dtype) for x in ins[:9]] + [pltpu.SemaphoreType.DMA((12 + here,))],
        compiler_params=params(24),
        cost_estimate=cost(2 * count * rows * fwidth + 2 * here * count * fwidth * hidden, 3 * 10**6,
                           here * count * hidden),
        name="route",
    )(*in_hbm(ins))
    far = swap(far)
    other_both = swap(own_both)
    next_segment = lax.ppermute(segment, "rows", [(i, i ^ 1) for i in range(n)])
    other_segment = swap(segment)

    ins = (cls_token, attn_gain, pred_scale, pred_shift, feat_bias, ffn_gain, own_qkv, other_qkv, index)
    table, where, place = pl.pallas_call(
        constants_kernel,
        out_shape=[shape((TABLE, width), F32), shape((count, 3), jnp.int32), shape((1, dealt), jnp.int32)],
        in_specs=[VMEM] * len(ins),
        out_specs=[VMEM] * 3,
        compiler_params=params(16),
        cost_estimate=cost(10**8, 2 * 10**6),
        name="constants",
    )(*ins)

    local = qkv_weight.shape[2]
    sent = pl.pallas_call(
        functools.partial(attend_kernel, members),
        out_shape=[shape((slots // blocks, 2 * local), BF)] * blocks,
        in_specs=[VMEM] * 9,
        out_specs=[VMEM] * blocks,
        compiler_params=params(24),
        cost_estimate=cost(10**9, 2 * 10**6),
        name="attend",
    )(mine, near, far, place, table, own_both, other_both, own_qkv, other_qkv)

    def across(x, k):
        return lax.ppermute(x, "rows", [(i, i ^ (2 * k)) for i in range(n)])

    def exchange(x):
        groups = [[2 * q + b for q in range(pairs)] for b in range(2)]
        return lax.all_to_all(x, "rows", split_axis=0, concat_axis=0, axis_index_groups=groups, tiled=True)

    if relative:
        got = [sent[0]] + [across(sent[k], k) for k in range(1, pairs)]
    else:
        got = exchange(sent[0].reshape(pairs, 2, half, 2 * local))
        got = [got.transpose(1, 0, 2, 3).reshape(slots, 2 * local)]

    tile = min(rows, 256)
    tiles = rows // tile

    def ensemble(first, number, after, held=()):
        return pl.pallas_call(
            functools.partial(ensemble_kernel, first, number, tile),
            out_shape=[shape((number * tile // LANES, LANES), F32)] + [shape(x.shape, x.dtype) for x in held],
            in_specs=[VMEM] * 4 + [ANY] * (1 + len(held)),
            out_specs=[VMEM] * (1 + len(held)),
            scratch_shapes=[pltpu.SemaphoreType.DMA((len(held),))] if held else [],
            compiler_params=params(24),
            cost_estimate=cost(2 * here * number * tile * fwidth * hidden, 10**6, here * number * tile * hidden),
            name="ensemble",
        )(features, member_in, member_bias, member_out, after, *held)

    early = (tiles + 1) // 2
    preds, table, both0, both1, up0, up1 = ensemble(
        0, early, sent[0], (table, own_both, other_both, segment, other_segment))
    preds = [preds]

    state, next_rows = pl.pallas_call(
        functools.partial(arrive_kernel, blocks, half),
        out_shape=[shape((slots // 2, width), F32), shape((slots // 2, width), BF)],
        in_specs=[VMEM] * (blocks + 3),
        out_specs=[VMEM] * 2,
        compiler_params=params(24),
        cost_estimate=cost(2 * 10**8, 2 * 10**6),
        name="arrive",
    )(*got[::-1], table, both0, both1)
    other_rows = swap(next_rows)
    near_scores, up2 = pl.pallas_call(
        functools.partial(near_score_kernel, blocks, half),
        out_shape=[shape((slots // 2, 1), F32), shape(next_segment.shape, BF)],
        in_specs=[VMEM] * (blocks + 5) + [ANY],
        out_specs=[VMEM] * 2,
        scratch_shapes=[pltpu.SemaphoreType.DMA((1,))],
        compiler_params=params(24),
        cost_estimate=cost(5 * 10**8, 2 * 10**6),
        name="near_score",
    )(*got[::-1], table, both0, both1, up0, up1, next_segment)
    scores = pl.pallas_call(
        functools.partial(far_score_kernel, blocks, half),
        out_shape=shape((blocks, LANES if relative else 3 * slots // 2), F32),
        in_specs=[VMEM] * 5,
        out_specs=VMEM,
        compiler_params=params(24),
        cost_estimate=cost(2 * 10**8, 10**6),
        name="far_score",
    )(near_scores, state, next_rows, other_rows, up2)
    for first in range(early, tiles):
        preds += ensemble(first, 1, scores)
    back = scores
    if relative:
        step = 1
        while step < pairs:
            back = jnp.concatenate([back, across(back, step)], axis=0)
            step *= 2
    else:
        back = exchange(back.reshape(3, pairs, half).transpose(1, 0, 2)).reshape(pairs, 3 * half)
        back = jnp.pad(back, ((0, 0), (0, LANES - 3 * half)))
    lines = back.shape[0]
    near_lines = jnp.concatenate([back, *preds], axis=0)
    line_of, lane_of = pl.pallas_call(
        functools.partial(expand_kernel, 2 * lines),
        out_shape=[shape((6 * lines, rows), BF), shape((1, rows), jnp.int32)],
        in_specs=[VMEM, ANY],
        out_specs=[VMEM] * 2,
        compiler_params=params(16),
        cost_estimate=cost(10**8, 10**6),
        name="expand",
    )(where, preds[-1])

    final = pl.pallas_call(
        functools.partial(finish_kernel, members, half, lines),
        out_shape=shape((1, rows), F32),
        in_specs=[VMEM] * 4,
        out_specs=VMEM,
        compiler_params=params(8),
        cost_estimate=cost(10**6, 10**6),
        name="finish",
    )(line_of, lane_of, near_lines, swap(near_lines))
    return final.reshape(rows)


def solution(mesh):
    placed = (
        P(("groups", "rows"), None),
        P(("groups", "rows"), None),
        P(("groups", "rows"), None, None),
        P("member", None, None),
        P("member", None),
        P("member", None),
        P("member", None),
        P(),
        P(),
        P(),
        P(),
        P(),
        P(None, None, "member"),
        P("member", None),
        P(),
        P("rows", None, "member"),
        P("rows", "member"),
        P("rows", "member", None),
        P("rows", None),
    )
    return jax.shard_map(
        per_device, mesh=mesh, in_specs=placed, out_specs=P(("groups", "rows")), check_vma=False
    )
```

profile of v0, /device:TPU:0, one launch (start us, length us, event | category | flops | bytes accessed | tf_op | source)
XLA Modules:
  0.0 33.2 jit_solution(3802186873052357410)
XLA Ops:
  0.0 0.5 %collective-permute-start = (bf16[3,512,256]{2,1,0:T(8,128)(2,1)}, bf16[3,512,256]{2,1,0:T(8,128)(2,1)S(1)}, u32[]{:S(2)}, u32[]{:S(2)}) collective-permute-start(bf16[3,512,256]{2,1,0:T(8,128)(2,1)} %qkv_hbm.1), channel_id=1, source_target_pairs={{0,1},{1,0},{2,3},{3,2},{4,5},{5,4},{6,7},{7,6},{8,9},{9,8},{10,11... | collective-permute-start | bytes 2359304 | tf_op jit(solution)/shard_map/ppermute | solution.py:387
  0.5 4.0 %route.1 = (s32[8,256]{1,0:T(8,128)S(1)}, bf16[128,512]{1,0:T(8,128)(2,1)S(1)}, bf16[128,128]{1,0:T(8,128)(2,1)S(1)}, bf16[128,128]{1,0:T(8,128)(2,1)S(1)}, bf16...) custom-call(s32[1,256]{1,0:T(1,128)} %esc_hbm.1, s32[1,256]{1,0:T(1,128)} %bitcast.10, ...), custom_call_target="tpu_custom_call" | custom-call | flops 805306368 | bytes 3000000 | tf_op jit(solution)/shard_map/route/pallas_call | solution.py:401
  4.6 0.4 %collective-permute-start.6 = (bf16[528,512]{1,0:T(8,128)(2,1)S(1)}, bf16[528,512]{1,0:T(8,128)(2,1)S(1)}, u32[]{:S(2)}, u32[]{:S(2)}) collective-permute-start(bf16[528,512]{1,0:T(8,128)(2,1)S(1)} %get-tuple-element.44.refs_3_), channel_id=1, source_target_pairs={{0,1},{1,0},{2,3},{3,2},{4,5},{5,4},{6,7},{7,6},{8,9},{9,8},{10,11... | collective-permute-start | bytes 1622024 | tf_op jit(solution)/shard_map/ppermute | solution.py:387
  5.1 2.6 %collective-permute-start.7 = (bf16[528,512]{1,0:T(8,128)(2,1)S(1)}, bf16[528,512]{1,0:T(8,128)(2,1)S(1)}, u32[]{:S(2)}, u32[]{:S(2)}) collective-permute-start(bf16[528,512]{1,0:T(8,128)(2,1)S(1)} %get-tuple-element.44.refs_3_), channel_id=1, source_target_pairs={{0,2},{2,0},{4,6},{6,4},{8,10},{10,8},{12,14},{14,12},{1,3},{3,1},... | collective-permute-start | bytes 1622024 | tf_op jit(solution)/shard_map/ppermute | solution.py:416
  7.9 0.7 %constants.1 = (f32[40,512]{1,0:T(8,128)S(1)}, s32[256,3]{1,0:T(8,128)S(1)}, s32[1,128]{1,0:T(1,128)S(1)}) custom-call(f32[1,512]{1,0:T(1,128)S(1)} %bitcast.6, f32[1,512]{1,0:T(1,128)S(1)} %bitcast.7, f32[4,512]{1,0:T(4,128)S(1)} %copy-done.4, f32[4,512]{1,0:T(4,128)S(1)} %copy-done.5, f32[1,512]{1,0:T(1,128)S(1)} %bitcast.8, f32[1,512]{1,0:T(1,128)S(1)} %bitcast.9, ...), custom_call_target="tpu_custom_call" | custom-call | flops 100000000 | bytes 2000000 | tf_op jit(solution)/shard_map/constants/pallas_call | solution.py:420
  8.7 0.2 collective-permute-done.1.far_ref
  8.9 2.1 %attend.1 = (bf16[64,512]{1,0:T(8,128)(2,1)S(1)}, bf16[64,512]{1,0:T(8,128)(2,1)S(1)}, bf16[64,512]{1,0:T(8,128)(2,1)S(1)}, bf16[64,512]{1,0:T(8,128)(2,1)S(1)}) custom-call(bf16[128,512]{1,0:T(8,128)(2,1)S(1)} %get-tuple-element.34.rows_ref, bf16[128,128]{1,0:T(8,128)(2,1)S(1)} %get-tuple-element.35.near_ref, ...), custom_call_target="tpu_custom_call" | custom-call | flops 1000000000 | bytes 2000000 | tf_op jit(solution)/shard_map/attend/pallas_call | solution.py:431
  11.0 3.7 %collective-permute-start.3 = (bf16[64,512]{1,0:T(8,128)(2,1)S(1)}, bf16[64,512]{1,0:T(8,128)(2,1)S(1)}, u32[]{:S(2)}, u32[]{:S(2)}) collective-permute-start(bf16[64,512]{1,0:T(8,128)(2,1)S(1)} %get-tuple-element.40), channel_id=1, source_target_pairs={{0,12},{2,14},{4,8},{6,10},{8,4},{10,6},{12,0},{14,2},{1,13},{3,15... | collective-permute-start | bytes 196616 | tf_op jit(solution)/shard_map/ppermute | solution.py:442
  14.7 0.8 %collective-permute-start.5 = (bf16[64,512]{1,0:T(8,128)(2,1)S(1)}, bf16[64,512]{1,0:T(8,128)(2,1)S(1)}, u32[]{:S(2)}, u32[]{:S(2)}) collective-permute-start(bf16[64,512]{1,0:T(8,128)(2,1)S(1)} %get-tuple-element.42), channel_id=1, source_target_pairs={{0,4},{2,6},{4,0},{6,2},{8,12},{10,14},{12,8},{14,10},{1,5},{3,7},... | collective-permute-start | bytes 196616 | tf_op jit(solution)/shard_map/ppermute | solution.py:442
  15.5 2.4 %ensemble.3 = (f32[4,128]{1,0:T(4,128)S(1)}, f32[40,512]{1,0:T(8,128)S(1)}, bf16[512,512]{1,0:T(8,128)(2,1)S(1)}, bf16[512,512]{1,0:T(8,128)(2,1)S(1)}, bf16[528...) custom-call(bf16[1024,512]{1,0:T(8,128)(2,1)S(1)} %copy-done.1, bf16[2,512,1024]{2,1,0:T(8,128)(2,1)S(1)} %copy-done, ...), custom_call_target="tpu_custom_call" | custom-call | flops 1073741824 | bytes 1000000 | tf_op jit(solution)/shard_map/ensemble/pallas_call | solution.py:458
  17.9 2.6 %collective-permute-done.4.refs_1_ = bf16[64,512]{1,0:T(8,128)(2,1)S(1)} collective-permute-done((bf16[64,512]{1,0:T(8,128)(2,1)S(1)}, bf16[64,512]{1,0:T(8,128)(2,1)S(1)}, u32[]{:S(2)}, u32[]{:S(2)}) %collective-permute-start.4) | collective-permute-done | bytes 65568 | tf_op jit(solution)/shard_map/ppermute | solution.py:442
  20.6 0.4 %arrive.1 = (f32[128,512]{1,0:T(8,128)S(1)}, bf16[128,512]{1,0:T(8,128)(2,1)S(1)}) custom-call(bf16[64,512]{1,0:T(8,128)(2,1)S(1)} %collective-permute-done.3.refs_0_, bf16[64,512]{1,0:T(8,128)(2,1)S(1)} %collective-permute-done.4.refs_1_, bf16[64,512]{1,0:T(8,128)(2,1)S(1)} %collective-permute-done.5.refs_2_, ...), custom_call_target="tpu_custom_call" | custom-call | flops 200000000 | bytes 2000000 | tf_op jit(solution)/shard_map/arrive/pallas_call | solution.py:474
  21.1 0.8 %near_score.1 = (f32[128,1]{1,0:T(8,128)S(1)}, bf16[528,512]{1,0:T(8,128)(2,1)S(1)}) custom-call(bf16[64,512]{1,0:T(8,128)(2,1)S(1)} %collective-permute-done.3.refs_0_, bf16[64,512]{1,0:T(8,128)(2,1)S(1)} %collective-permute-done.4.refs_1_, bf16[64,512]{1,0:T(8,128)(2,1)S(1)} %collective-permute-done.5.refs_2_, ...), custom_call_target="tpu_custom_call" | custom-call | flops 500000000 | bytes 2000000 | tf_op jit(solution)/shard_map/near_score/pallas_call | solution.py:484
  21.9 0.5 %collective-permute-done.8.other_ref = bf16[128,512]{1,0:T(8,128)(2,1)S(1)} collective-permute-done((bf16[128,512]{1,0:T(8,128)(2,1)S(1)}, bf16[128,512]{1,0:T(8,128)(2,1)S(1)}, u32[]{:S(2)}, u32[]{:S(2)}) %collective-permute-start.8) | collective-permute-done | bytes 131104 | tf_op jit(solution)/shard_map/ppermute | solution.py:387
  22.4 0.4 %far_score.1.after_ref = f32[4,128]{1,0:T(4,128)S(1)} custom-call(f32[128,1]{1,0:T(8,128)S(1)} %get-tuple-element.50.near_ref, f32[128,512]{1,0:T(8,128)S(1)} %get-tuple-element.51.state_ref, bf16[128,512]{1,0:T(8,128)(2,1)S(1)} %get-tuple-element.52.mine_ref, bf16[128,512]{1,0:T(8,128)(2,1)S(1)} %collective-permute-done.8.other_ref, ...), custom_call_target="tpu_custom_call" | custom-call | flops 200000000 | bytes 1000000 | tf_op jit(solution)/shard_map/far_score/pallas_call | solution.py:494
  22.8 1.2 %collective-permute-start.9 = (f32[4,128]{1,0:T(4,128)S(1)}, f32[4,128]{1,0:T(4,128)S(1)}, u32[]{:S(2)}, u32[]{:S(2)}) collective-permute-start(f32[4,128]{1,0:T(4,128)S(1)} %far_score.1.after_ref), channel_id=1, source_target_pairs={{0,4},{2,6},{4,0},{6,2},{8,12},{10,14},{12,8},{14,10},{1,5},{3,7},... | collective-permute-start | bytes 6152 | tf_op jit(solution)/shard_map/ppermute | solution.py:442
  24.0 1.1 %ensemble.4.after_ref = f32[2,128]{1,0:T(2,128)S(1)} custom-call(bf16[1024,512]{1,0:T(8,128)(2,1)S(1)} %copy-done.1, bf16[2,512,1024]{2,1,0:T(8,128)(2,1)S(1)} %copy-done, f32[2,1024]{1,0:T(2,128)S(1)} %copy-done.2, bf16[2,1024]{1,0:T(2,128)(2,1)S(1)} %copy-done.3, f32[4,128]{1,0:T(4,128)S(1)} %far_score.1.after_ref), custom_call_target="tpu_custom_call" | custom-call | flops 536870912 | bytes 1000000 | tf_op jit(solution)/shard_map/ensemble/pallas_call | solution.py:458
  25.2 1.3 %collective-permute-done.9 = f32[4,128]{1,0:T(4,128)S(1)} collective-permute-done((f32[4,128]{1,0:T(4,128)S(1)}, f32[4,128]{1,0:T(4,128)S(1)}, u32[]{:S(2)}, u32[]{:S(2)}) %collective-permute-start.9) | collective-permute-done | bytes 2080 | tf_op jit(solution)/shard_map/ppermute | solution.py:442
  26.5 1.8 %collective-permute-start.10 = (f32[8,128]{1,0:T(8,128)S(1)}, f32[8,128]{1,0:T(8,128)S(1)}, u32[]{:S(2)}, u32[]{:S(2)}) collective-permute-start(f32[8,128]{1,0:T(8,128)S(1)} %pad_maximum_fusion), channel_id=1, source_target_pairs={{0,8},{2,10},{4,12},{6,14},{8,0},{10,2},{12,4},{14,6},{1,9},{3,11}... | collective-permute-start | bytes 12296 | tf_op jit(solution)/shard_map/ppermute | solution.py:442
  28.3 1.1 %ensemble.5 = f32[2,128]{1,0:T(2,128)S(1)} custom-call(bf16[1024,512]{1,0:T(8,128)(2,1)S(1)} %copy-done.1, bf16[2,512,1024]{2,1,0:T(8,128)(2,1)S(1)} %copy-done, f32[2,1024]{1,0:T(2,128)S(1)} %copy-done.2, bf16[2,1024]{1,0:T(2,128)(2,1)S(1)} %copy-done.3, f32[4,128]{1,0:T(4,128)S(1)} %far_score.1.after_ref), custom_call_target="tpu_custom_call" | custom-call | flops 536870912 | bytes 1000000 | tf_op jit(solution)/shard_map/ensemble/pallas_call | solution.py:458
  29.4 1.6 %collective-permute-done.10 = f32[8,128]{1,0:T(8,128)S(1)} collective-permute-done((f32[8,128]{1,0:T(8,128)S(1)}, f32[8,128]{1,0:T(8,128)S(1)}, u32[]{:S(2)}, u32[]{:S(2)}) %collective-permute-start.10) | collective-permute-done | bytes 4128 | tf_op jit(solution)/shard_map/ppermute | solution.py:442
  31.1 0.4 %expand.1 = (bf16[96,1024]{1,0:T(8,128)(2,1)S(1)}, s32[1,1024]{1,0:T(1,128)S(1)}) custom-call(s32[256,3]{1,0:T(8,128)S(1)} %get-tuple-element.33.where_ref, f32[2,128]{1,0:T(2,128)S(1)} %ensemble.4.after_ref), custom_call_target="tpu_custom_call" | custom-call | flops 100000000 | bytes 1000000 | tf_op jit(solution)/shard_map/expand/pallas_call | solution.py:516
  31.6 0.7 %collective-permute-done.11.far_ref = f32[24,128]{1,0:T(8,128)S(1)} collective-permute-done((f32[24,128]{1,0:T(8,128)S(1)}, f32[24,128]{1,0:T(8,128)S(1)}, u32[]{:S(2)}, u32[]{:S(2)}) %collective-permute-start.11) | collective-permute-done | bytes 12320 | tf_op jit(solution)/shard_map/ppermute | solution.py:387
  32.3 0.9 %finish.1 = f32[1,1024]{1,0:T(1,128)} custom-call(bf16[96,1024]{1,0:T(8,128)(2,1)S(1)} %get-tuple-element.54.line_ref, s32[1,1024]{1,0:T(1,128)S(1)} %get-tuple-element.55.lane_ref, f32[24,128]{1,0:T(8,128)S(1)} %concatenate.8.near_ref, f32[24,128]{1,0:T(8,128)S(1)} %collective-permute-done.11.far_ref), custom_call_target="tpu_custom_call" | custom-call | flops 1000000 | bytes 1000000 | tf_op jit(solution)/shard_map/finish/pallas_call | solution.py:526
  (33 shorter events, 0.5 us)
Async XLA Ops:
  0.0 7.8 %collective-permute-start = (bf16[3,512,256]{2,1,0:T(8,128)(2,1)}, bf16[3,512,256]{2,1,0:T(8,128)(2,1)S(1)}, u32[]{:S(2)}, u32[]{:S(2)}) collective-permute-start(bf16[3,512,256]{2,1,0:T(8,128)(2,1)} %qkv_hbm.1), channel_id=1, source_target_pairs={{0,1},{1,0},{2,3},{3,2},{4,5},{5,4},{6,7},{7,6},{8,9},{9,8},{10,11... | collective-permute-start | bytes 2359304 | tf_op jit(solution)/shard_map/ppermute | solution.py:387
  0.5 7.4 %copy-start.4 = (f32[4,512]{1,0:T(4,128)S(1)}, f32[4,512]{1,0:T(4,128)}, u32[]{:S(2)}) copy-start(f32[4,512]{1,0:T(4,128)} %scale_ref.1) | copy-start | bytes 24580
  0.5 7.4 %copy-start.5 = (f32[4,512]{1,0:T(4,128)S(1)}, f32[4,512]{1,0:T(4,128)}, u32[]{:S(2)}) copy-start(f32[4,512]{1,0:T(4,128)} %shift_ref.1) | copy-start | bytes 24580
  0.5 7.4 %copy-start.6 = (f32[512]{0:T(512)S(1)}, f32[512]{0:T(512)}, u32[]{:S(2)}) copy-start(f32[512]{0:T(512)} %param.29) | copy-start | bytes 6148
  0.5 7.4 %copy-start.7 = (f32[512]{0:T(512)S(1)}, f32[512]{0:T(512)}, u32[]{:S(2)}) copy-start(f32[512]{0:T(512)} %param.30) | copy-start | bytes 6148
  0.5 7.4 %copy-start.8 = (f32[512]{0:T(512)S(1)}, f32[512]{0:T(512)}, u32[]{:S(2)}) copy-start(f32[512]{0:T(512)} %param.26) | copy-start | bytes 6148
  0.5 7.4 %copy-start.9 = (f32[512]{0:T(512)S(1)}, f32[512]{0:T(512)}, u32[]{:S(2)}) copy-start(f32[512]{0:T(512)} %param.33) | copy-start | bytes 6148
  4.5 4.4 %collective-permute-start.2 = (bf16[512,512]{1,0:T(8,128)(2,1)S(1)}, bf16[512,512]{1,0:T(8,128)(2,1)S(1)}, u32[]{:S(2)}, u32[]{:S(2)}) collective-permute-start(bf16[512,512]{1,0:T(8,128)(2,1)S(1)} %get-tuple-element.39.fw0_ref.refs_1_), channel_id=1, source_target_pairs={{0,1},{1,0},{2,3},{3,2},{4,5},{5,4},{6,7},{7,6},{8,9},{9,8},{10,11... | collective-permute-start | bytes 1572872 | tf_op jit(solution)/shard_map/ppermute | solution.py:387
  4.6 10.8 %collective-permute-start.6 = (bf16[528,512]{1,0:T(8,128)(2,1)S(1)}, bf16[528,512]{1,0:T(8,128)(2,1)S(1)}, u32[]{:S(2)}, u32[]{:S(2)}) collective-permute-start(bf16[528,512]{1,0:T(8,128)(2,1)S(1)} %get-tuple-element.44.refs_3_), channel_id=1, source_target_pairs={{0,1},{1,0},{2,3},{3,2},{4,5},{5,4},{6,7},{7,6},{8,9},{9,8},{10,11... | collective-permute-start | bytes 1622024 | tf_op jit(solution)/shard_map/ppermute | solution.py:387
  5.1 16.0 %collective-permute-start.7 = (bf16[528,512]{1,0:T(8,128)(2,1)S(1)}, bf16[528,512]{1,0:T(8,128)(2,1)S(1)}, u32[]{:S(2)}, u32[]{:S(2)}) collective-permute-start(bf16[528,512]{1,0:T(8,128)(2,1)S(1)} %get-tuple-element.44.refs_3_), channel_id=1, source_target_pairs={{0,2},{2,0},{4,6},{6,4},{8,10},{10,8},{12,14},{14,12},{1,3},{3,1},... | collective-permute-start | bytes 1622024 | tf_op jit(solution)/shard_map/ppermute | solution.py:416
  7.7 1.2 %collective-permute-start.1 = (bf16[128,128]{1,0:T(8,128)(2,1)S(1)}, bf16[128,128]{1,0:T(8,128)(2,1)S(1)}, u32[]{:S(2)}, u32[]{:S(2)}) collective-permute-start(bf16[128,128]{1,0:T(8,128)(2,1)S(1)} %get-tuple-element.36), channel_id=1, source_target_pairs={{0,1},{1,0},{2,3},{3,2},{4,5},{5,4},{6,7},{7,6},{8,9},{9,8},{10,11... | collective-permute-start | bytes 98312 | tf_op jit(solution)/shard_map/ppermute | solution.py:387
  8.6 6.9 %copy-start = (bf16[2,512,1024]{2,1,0:T(8,128)(2,1)S(1)}, bf16[2,512,1024]{2,1,0:T(8,128)(2,1)}, u32[]{:S(2)}) copy-start(bf16[2,512,1024]{2,1,0:T(8,128)(2,1)} %w_ref.5) | copy-start | bytes 6291460
  8.6 6.8 %copy-start.1 = (bf16[1024,512]{1,0:T(8,128)(2,1)S(1)}, bf16[1024,512]{1,0:T(8,128)(2,1)}, u32[]{:S(2)}) copy-start(bf16[1024,512]{1,0:T(8,128)(2,1)} %feat_ref.5) | copy-start | bytes 3145732
  8.6 6.8 %copy-start.2 = (f32[2,1024]{1,0:T(2,128)S(1)}, f32[2,1024]{1,0:T(2,128)}, u32[]{:S(2)}) copy-start(f32[2,1024]{1,0:T(2,128)} %bias_ref.5) | copy-start | bytes 24580
  8.7 6.8 %copy-start.3 = (bf16[2,1024]{1,0:T(2,128)(2,1)S(1)}, bf16[2,1024]{1,0:T(2,128)(2,1)}, u32[]{:S(2)}) copy-start(bf16[2,1024]{1,0:T(2,128)(2,1)} %out_ref.5) | copy-start | bytes 12292
  11.0 6.9 %collective-permute-start.3 = (bf16[64,512]{1,0:T(8,128)(2,1)S(1)}, bf16[64,512]{1,0:T(8,128)(2,1)S(1)}, u32[]{:S(2)}, u32[]{:S(2)}) collective-permute-start(bf16[64,512]{1,0:T(8,128)(2,1)S(1)} %get-tuple-element.40), channel_id=1, source_target_pairs={{0,12},{2,14},{4,8},{6,10},{8,4},{10,6},{12,0},{14,2},{1,13},{3,15... | collective-permute-start | bytes 196616 | tf_op jit(solution)/shard_map/ppermute | solution.py:442
  14.7 5.9 %collective-permute-start.4 = (bf16[64,512]{1,0:T(8,128)(2,1)S(1)}, bf16[64,512]{1,0:T(8,128)(2,1)S(1)}, u32[]{:S(2)}, u32[]{:S(2)}) collective-permute-start(bf16[64,512]{1,0:T(8,128)(2,1)S(1)} %get-tuple-element.41), channel_id=1, source_target_pairs={{0,8},{2,10},{4,12},{6,14},{8,0},{10,2},{12,4},{14,6},{1,9},{3,11}... | collective-permute-start | bytes 196616 | tf_op jit(solution)/shard_map/ppermute | solution.py:442
  14.7 5.9 %collective-permute-start.5 = (bf16[64,512]{1,0:T(8,128)(2,1)S(1)}, bf16[64,512]{1,0:T(8,128)(2,1)S(1)}, u32[]{:S(2)}, u32[]{:S(2)}) collective-permute-start(bf16[64,512]{1,0:T(8,128)(2,1)S(1)} %get-tuple-element.42), channel_id=1, source_target_pairs={{0,4},{2,6},{4,0},{6,2},{8,12},{10,14},{12,8},{14,10},{1,5},{3,7},... | collective-permute-start | bytes 196616 | tf_op jit(solution)/shard_map/ppermute | solution.py:442
  21.0 1.4 %collective-permute-start.8 = (bf16[128,512]{1,0:T(8,128)(2,1)S(1)}, bf16[128,512]{1,0:T(8,128)(2,1)S(1)}, u32[]{:S(2)}, u32[]{:S(2)}) collective-permute-start(bf16[128,512]{1,0:T(8,128)(2,1)S(1)} %get-tuple-element.52.mine_ref), channel_id=1, source_target_pairs={{0,1},{1,0},{2,3},{3,2},{4,5},{5,4},{6,7},{7,6},{8,9},{9,8},{10,11... | collective-permute-start | bytes 393224 | tf_op jit(solution)/shard_map/ppermute | solution.py:387
  22.8 3.7 %collective-permute-start.9 = (f32[4,128]{1,0:T(4,128)S(1)}, f32[4,128]{1,0:T(4,128)S(1)}, u32[]{:S(2)}, u32[]{:S(2)}) collective-permute-start(f32[4,128]{1,0:T(4,128)S(1)} %far_score.1.after_ref), channel_id=1, source_target_pairs={{0,4},{2,6},{4,0},{6,2},{8,12},{10,14},{12,8},{14,10},{1,5},{3,7},... | collective-permute-start | bytes 6152 | tf_op jit(solution)/shard_map/ppermute | solution.py:442
  26.5 4.5 %collective-permute-start.10 = (f32[8,128]{1,0:T(8,128)S(1)}, f32[8,128]{1,0:T(8,128)S(1)}, u32[]{:S(2)}, u32[]{:S(2)}) collective-permute-start(f32[8,128]{1,0:T(8,128)S(1)} %pad_maximum_fusion), channel_id=1, source_target_pairs={{0,8},{2,10},{4,12},{6,14},{8,0},{10,2},{12,4},{14,6},{1,9},{3,11}... | collective-permute-start | bytes 12296 | tf_op jit(solution)/shard_map/ppermute | solution.py:442
  31.0 1.2 %collective-permute-start.11 = (f32[24,128]{1,0:T(8,128)S(1)}, f32[24,128]{1,0:T(8,128)S(1)}, u32[]{:S(2)}, u32[]{:S(2)}) collective-permute-start(f32[24,128]{1,0:T(8,128)S(1)} %concatenate.8.near_ref), channel_id=1, source_target_pairs={{0,1},{1,0},{2,3},{3,2},{4,5},{5,4},{6,7},{7,6},{8,9},{9,8},{10,11... | collective-permute-start | bytes 36872 | tf_op jit(solution)/shard_map/ppermute | solution.py:387
where the time goes:
time: 33.3 us; the launch traced here: 33.2 us
  Pallas kernels  14.6 us (44%)
  starting transfers between devices  11.3 us (34%)
  waiting for transfers between devices  6.96 us (21%)
    ppermute x5, starting transfers between devices, across(): return lax.ppermute(x, 'rows', [(i, i ^ 2 * k) for i in range(n)])  7.44 us
    ppermute x5, waiting for transfers between devices, across(): return lax.ppermute(x, 'rows', [(i, i ^ 2 * k) for i in range(n)])  5.54 us
    pallas_call x3, Pallas kernels, ensemble(): pl.pallas_call(functools.partial(ensemble_kernel, first, number, tile), o...  4.69 us
    pallas_call x1, Pallas kernels, per_device(): pl.pallas_call(functools.partial(route_kernel, n, half, relative), out_sh...  4.01 us
    ppermute x1, starting transfers between devices, per_device(): next_segment = lax.ppermute(segment, 'rows', [(i, i ^ 1) for i in range(n)])  2.57 us
    pallas_call x1, Pallas kernels, per_device(): pl.pallas_call(functools.partial(attend_kernel, members), out_shape=[shap...  2.14 us
    ppermute x6, waiting for transfers between devices, swap(): return lax.ppermute(x, 'member', [(0, 1), (1, 0)])  1.42 us
    ppermute x6, starting transfers between devices, swap(): return lax.ppermute(x, 'member', [(0, 1), (1, 0)])  1.33 us
  transfers between devices with their start and end apart: 12, of which 6 were waited for; matrix products, arithmetic and copies ran while one was open for 0% of the time, Pallas kernels for 40%

commit v1 on v0

--- a/solution.py
+++ b/solution.py
@@ -291,15 +291,13 @@
 
 
 def near_score_kernel(blocks, half, *refs):
-    table_ref, both0_ref, both1_ref, up0_ref, up1_ref, next_hbm, score_ref, next_ref, sems = refs[blocks:]
-    (copy,) = start_all([(next_hbm, next_ref)], sems)
+    table_ref, both0_ref, both1_ref, up0_ref, up1_ref, score_ref = refs[blocks:]
     state, normed = states(arrived(refs[:blocks][::-1], half, 0), table_ref, both0_ref, both1_ref)
     up, down, bias, head = unpack(up0_ref)
     terms = state * head + hidden_terms(normed, up, down, bias)
     up, down, bias, _ = unpack(up1_ref)
     terms = terms + hidden_terms(normed, up, down, bias)
     score_ref[...] = jnp.sum(terms, axis=-1, keepdims=True)
-    copy.wait()
 
 
 def far_score_kernel(blocks, half, near_ref, state_ref, mine_ref, other_ref, up2_ref, out_ref):
@@ -481,16 +479,15 @@
         name="arrive",
     )(*got[::-1], table, both0, both1)
     other_rows = swap(next_rows)
-    near_scores, up2 = pl.pallas_call(
+    near_scores = pl.pallas_call(
         functools.partial(near_score_kernel, blocks, half),
-        out_shape=[shape((slots // 2, 1), F32), shape(next_segment.shape, BF)],
-        in_specs=[VMEM] * (blocks + 5) + [ANY],
-        out_specs=[VMEM] * 2,
-        scratch_shapes=[pltpu.SemaphoreType.DMA((1,))],
+        out_shape=shape((slots // 2, 1), F32),
+        in_specs=[VMEM] * (blocks + 5),
+        out_specs=VMEM,
         compiler_params=params(24),
         cost_estimate=cost(5 * 10**8, 2 * 10**6),
         name="near_score",
-    )(*got[::-1], table, both0, both1, up0, up1, next_segment)
+    )(*got[::-1], table, both0, both1, up0, up1)
     scores = pl.pallas_call(
         functools.partial(far_score_kernel, blocks, half),
         out_shape=shape((blocks, LANES if relative else 3 * slots // 2), F32),
@@ -499,7 +496,7 @@
         compiler_params=params(24),
         cost_estimate=cost(2 * 10**8, 10**6),
         name="far_score",
-    )(near_scores, state, next_rows, other_rows, up2)
+    )(near_scores, state, next_rows, other_rows, next_segment)
     for first in range(early, tiles):
         preds += ensemble(first, 1, scores)
     back = scores

time: 33.3 us -> 33.3 us (level)
  waiting for transfers between devices: 6.96 us -> 7.53 us
  starting transfers between devices: 11.3 us -> 10.9 us
    ppermute x5, waiting for transfers between devices: 5.54 us -> 6.03 us  [across(): return lax.ppermute(x, 'rows', [(i, i ^ 2 * k) for i in range(n)])]
    ppermute x5, starting transfers between devices: 7.44 us -> 6.95 us  [across(): return lax.ppermute(x, 'rows', [(i, i ^ 2 * k) for i in range(n)])]
where the time goes in v1:
time: 33.3 us; the launch traced here: 33.2 us
  Pallas kernels  14.5 us (44%)
  starting transfers between devices  10.9 us (33%)
  waiting for transfers between devices  7.53 us (23%)
    ppermute x5, starting transfers between devices, across(): return lax.ppermute(x, 'rows', [(i, i ^ 2 * k) for i in range(n)])  6.95 us
    ppermute x5, waiting for transfers between devices, across(): return lax.ppermute(x, 'rows', [(i, i ^ 2 * k) for i in range(n)])  6.03 us
    pallas_call x3, Pallas kernels, ensemble(): pl.pallas_call(functools.partial(ensemble_kernel, first, number, tile), o...  4.69 us
    pallas_call x1, Pallas kernels, per_device(): pl.pallas_call(functools.partial(route_kernel, n, half, relative), out_sh...  4.01 us
    ppermute x1, starting transfers between devices, per_device(): next_segment = lax.ppermute(segment, 'rows', [(i, i ^ 1) for i in range(n)])  2.57 us
    pallas_call x1, Pallas kernels, per_device(): pl.pallas_call(functools.partial(attend_kernel, members), out_shape=[shap...  2.13 us
    ppermute x6, waiting for transfers between devices, swap(): return lax.ppermute(x, 'member', [(0, 1), (1, 0)])  1.5 us
    ppermute x6, starting transfers between devices, swap(): return lax.ppermute(x, 'member', [(0, 1), (1, 0)])  1.33 us
  transfers between devices with their start and end apart: 12, of which 6 were waited for; matrix products, arithmetic and copies ran while one was open for 0% of the time, Pallas kernels for 40%

profile of v1, /device:TPU:0, one launch (start us, length us, event | category | flops | bytes accessed | tf_op | source)
XLA Modules:
  0.0 33.2 jit_solution(10261243290921058882)
XLA Ops:
  0.0 0.5 %collective-permute-start = (bf16[3,512,256]{2,1,0:T(8,128)(2,1)}, bf16[3,512,256]{2,1,0:T(8,128)(2,1)S(1)}, u32[]{:S(2)}, u32[]{:S(2)}) collective-permute-start(bf16[3,512,256]{2,1,0:T(8,128)(2,1)} %qkv_hbm.1), channel_id=1, source_target_pairs={{0,1},{1,0},{2,3},{3,2},{4,5},{5,4},{6,7},{7,6},{8,9},{9,8},{10,11... | collective-permute-start | bytes 2359304 | tf_op jit(solution)/shard_map/ppermute | solution.py:385
  0.5 4.0 %route.1 = (s32[8,256]{1,0:T(8,128)S(1)}, bf16[128,512]{1,0:T(8,128)(2,1)S(1)}, bf16[128,128]{1,0:T(8,128)(2,1)S(1)}, bf16[128,128]{1,0:T(8,128)(2,1)S(1)}, bf16...) custom-call(s32[1,256]{1,0:T(1,128)} %esc_hbm.1, s32[1,256]{1,0:T(1,128)} %bitcast.10, ...), custom_call_target="tpu_custom_call" | custom-call | flops 805306368 | bytes 3000000 | tf_op jit(solution)/shard_map/route/pallas_call | solution.py:399
  4.6 0.4 %collective-permute-start.6 = (bf16[528,512]{1,0:T(8,128)(2,1)S(1)}, bf16[528,512]{1,0:T(8,128)(2,1)S(1)}, u32[]{:S(2)}, u32[]{:S(2)}) collective-permute-start(bf16[528,512]{1,0:T(8,128)(2,1)S(1)} %get-tuple-element.42.refs_3_), channel_id=1, source_target_pairs={{0,1},{1,0},{2,3},{3,2},{4,5},{5,4},{6,7},{7,6},{8,9},{9,8},{10,11... | collective-permute-start | bytes 1622024 | tf_op jit(solution)/shard_map/ppermute | solution.py:385
  5.1 2.6 %collective-permute-start.8 = (bf16[528,512]{1,0:T(8,128)(2,1)S(1)}, bf16[528,512]{1,0:T(8,128)(2,1)S(1)}, u32[]{:S(2)}, u32[]{:S(2)}) collective-permute-start(bf16[528,512]{1,0:T(8,128)(2,1)S(1)} %get-tuple-element.42.refs_3_), channel_id=1, source_target_pairs={{0,2},{2,0},{4,6},{6,4},{8,10},{10,8},{12,14},{14,12},{1,3},{3,1},... | collective-permute-start | bytes 1622024 | tf_op jit(solution)/shard_map/ppermute | solution.py:414
  7.9 0.8 %constants.1 = (f32[40,512]{1,0:T(8,128)S(1)}, s32[256,3]{1,0:T(8,128)S(1)}, s32[1,128]{1,0:T(1,128)S(1)}) custom-call(f32[1,512]{1,0:T(1,128)S(1)} %bitcast.6, f32[1,512]{1,0:T(1,128)S(1)} %bitcast.7, f32[4,512]{1,0:T(4,128)S(1)} %copy-done.4, f32[4,512]{1,0:T(4,128)S(1)} %copy-done.5, f32[1,512]{1,0:T(1,128)S(1)} %bitcast.8, f32[1,512]{1,0:T(1,128)S(1)} %bitcast.9, ...), custom_call_target="tpu_custom_call" | custom-call | flops 100000000 | bytes 2000000 | tf_op jit(solution)/shard_map/constants/pallas_call | solution.py:418
  8.7 0.2 collective-permute-done.1.far_ref
  8.9 2.1 %attend.1 = (bf16[64,512]{1,0:T(8,128)(2,1)S(1)}, bf16[64,512]{1,0:T(8,128)(2,1)S(1)}, bf16[64,512]{1,0:T(8,128)(2,1)S(1)}, bf16[64,512]{1,0:T(8,128)(2,1)S(1)}) custom-call(bf16[128,512]{1,0:T(8,128)(2,1)S(1)} %get-tuple-element.32.rows_ref, bf16[128,128]{1,0:T(8,128)(2,1)S(1)} %get-tuple-element.33.near_ref, ...), custom_call_target="tpu_custom_call" | custom-call | flops 1000000000 | bytes 2000000 | tf_op jit(solution)/shard_map/attend/pallas_call | solution.py:429
  11.0 3.7 %collective-permute-start.3 = (bf16[64,512]{1,0:T(8,128)(2,1)S(1)}, bf16[64,512]{1,0:T(8,128)(2,1)S(1)}, u32[]{:S(2)}, u32[]{:S(2)}) collective-permute-start(bf16[64,512]{1,0:T(8,128)(2,1)S(1)} %get-tuple-element.38), channel_id=1, source_target_pairs={{0,12},{2,14},{4,8},{6,10},{8,4},{10,6},{12,0},{14,2},{1,13},{3,15... | collective-permute-start | bytes 196616 | tf_op jit(solution)/shard_map/ppermute | solution.py:440
  14.7 0.8 %collective-permute-start.5 = (bf16[64,512]{1,0:T(8,128)(2,1)S(1)}, bf16[64,512]{1,0:T(8,128)(2,1)S(1)}, u32[]{:S(2)}, u32[]{:S(2)}) collective-permute-start(bf16[64,512]{1,0:T(8,128)(2,1)S(1)} %get-tuple-element.40), channel_id=1, source_target_pairs={{0,4},{2,6},{4,0},{6,2},{8,12},{10,14},{12,8},{14,10},{1,5},{3,7},... | collective-permute-start | bytes 196616 | tf_op jit(solution)/shard_map/ppermute | solution.py:440
  15.5 2.4 %ensemble.3 = (f32[4,128]{1,0:T(4,128)S(1)}, f32[40,512]{1,0:T(8,128)S(1)}, bf16[512,512]{1,0:T(8,128)(2,1)S(1)}, bf16[512,512]{1,0:T(8,128)(2,1)S(1)}, bf16[528...) custom-call(bf16[1024,512]{1,0:T(8,128)(2,1)S(1)} %copy-done.1, bf16[2,512,1024]{2,1,0:T(8,128)(2,1)S(1)} %copy-done, ...), custom_call_target="tpu_custom_call" | custom-call | flops 1073741824 | bytes 1000000 | tf_op jit(solution)/shard_map/ensemble/pallas_call | solution.py:456
  17.9 2.6 %collective-permute-done.4.refs_1_ = bf16[64,512]{1,0:T(8,128)(2,1)S(1)} collective-permute-done((bf16[64,512]{1,0:T(8,128)(2,1)S(1)}, bf16[64,512]{1,0:T(8,128)(2,1)S(1)}, u32[]{:S(2)}, u32[]{:S(2)}) %collective-permute-start.4) | collective-permute-done | bytes 65568 | tf_op jit(solution)/shard_map/ppermute | solution.py:440
  20.6 0.4 %arrive.1 = (f32[128,512]{1,0:T(8,128)S(1)}, bf16[128,512]{1,0:T(8,128)(2,1)S(1)}) custom-call(bf16[64,512]{1,0:T(8,128)(2,1)S(1)} %collective-permute-done.3.refs_0_, bf16[64,512]{1,0:T(8,128)(2,1)S(1)} %collective-permute-done.4.refs_1_, bf16[64,512]{1,0:T(8,128)(2,1)S(1)} %collective-permute-done.5.refs_2_, ...), custom_call_target="tpu_custom_call" | custom-call | flops 200000000 | bytes 2000000 | tf_op jit(solution)/shard_map/arrive/pallas_call | solution.py:472
  21.1 0.7 %near_score.1.near_ref = f32[128,1]{1,0:T(8,128)S(1)} custom-call(bf16[64,512]{1,0:T(8,128)(2,1)S(1)} %collective-permute-done.3.refs_0_, bf16[64,512]{1,0:T(8,128)(2,1)S(1)} %collective-permute-done.4.refs_1_, bf16[64,512]{1,0:T(8,128)(2,1)S(1)} %collective-permute-done.5.refs_2_, bf16[64,512]{1,0:T(8,128)(2,1)S(1)} %get-tuple-element.41.after_ref.refs_3_, ...), custom_call_target="tpu_custom_call" | custom-call | flops 500000000 | bytes 2000000 | tf_op jit(solution)/shard_map/near_score/pallas_call | solution.py:482
  21.8 0.6 %collective-permute-done.7.other_ref = bf16[128,512]{1,0:T(8,128)(2,1)S(1)} collective-permute-done((bf16[128,512]{1,0:T(8,128)(2,1)S(1)}, bf16[128,512]{1,0:T(8,128)(2,1)S(1)}, u32[]{:S(2)}, u32[]{:S(2)}) %collective-permute-start.7) | collective-permute-done | bytes 131104 | tf_op jit(solution)/shard_map/ppermute | solution.py:385
  22.4 0.4 %far_score.1.after_ref = f32[4,128]{1,0:T(4,128)S(1)} custom-call(f32[128,1]{1,0:T(8,128)S(1)} %near_score.1.near_ref, f32[128,512]{1,0:T(8,128)S(1)} %get-tuple-element.48.state_ref, bf16[128,512]{1,0:T(8,128)(2,1)S(1)} %get-tuple-element.49.mine_ref, bf16[128,512]{1,0:T(8,128)(2,1)S(1)} %collective-permute-done.7.other_ref, ...), custom_call_target="tpu_custom_call" | custom-call | flops 200000000 | bytes 1000000 | tf_op jit(solution)/shard_map/far_score/pallas_call | solution.py:491
  22.8 1.2 %collective-permute-start.9 = (f32[4,128]{1,0:T(4,128)S(1)}, f32[4,128]{1,0:T(4,128)S(1)}, u32[]{:S(2)}, u32[]{:S(2)}) collective-permute-start(f32[4,128]{1,0:T(4,128)S(1)} %far_score.1.after_ref), channel_id=1, source_target_pairs={{0,4},{2,6},{4,0},{6,2},{8,12},{10,14},{12,8},{14,10},{1,5},{3,7},... | collective-permute-start | bytes 6152 | tf_op jit(solution)/shard_map/ppermute | solution.py:440
  24.0 1.1 %ensemble.4.after_ref = f32[2,128]{1,0:T(2,128)S(1)} custom-call(bf16[1024,512]{1,0:T(8,128)(2,1)S(1)} %copy-done.1, bf16[2,512,1024]{2,1,0:T(8,128)(2,1)S(1)} %copy-done, f32[2,1024]{1,0:T(2,128)S(1)} %copy-done.2, bf16[2,1024]{1,0:T(2,128)(2,1)S(1)} %copy-done.3, f32[4,128]{1,0:T(4,128)S(1)} %far_score.1.after_ref), custom_call_target="tpu_custom_call" | custom-call | flops 536870912 | bytes 1000000 | tf_op jit(solution)/shard_map/ensemble/pallas_call | solution.py:456
  25.1 1.3 %collective-permute-done.9 = f32[4,128]{1,0:T(4,128)S(1)} collective-permute-done((f32[4,128]{1,0:T(4,128)S(1)}, f32[4,128]{1,0:T(4,128)S(1)}, u32[]{:S(2)}, u32[]{:S(2)}) %collective-permute-start.9) | collective-permute-done | bytes 2080 | tf_op jit(solution)/shard_map/ppermute | solution.py:440
  26.5 1.3 %collective-permute-start.10 = (f32[8,128]{1,0:T(8,128)S(1)}, f32[8,128]{1,0:T(8,128)S(1)}, u32[]{:S(2)}, u32[]{:S(2)}) collective-permute-start(f32[8,128]{1,0:T(8,128)S(1)} %pad_maximum_fusion), channel_id=1, source_target_pairs={{0,8},{2,10},{4,12},{6,14},{8,0},{10,2},{12,4},{14,6},{1,9},{3,11}... | collective-permute-start | bytes 12296 | tf_op jit(solution)/shard_map/ppermute | solution.py:440
  27.8 1.1 %ensemble.5 = f32[2,128]{1,0:T(2,128)S(1)} custom-call(bf16[1024,512]{1,0:T(8,128)(2,1)S(1)} %copy-done.1, bf16[2,512,1024]{2,1,0:T(8,128)(2,1)S(1)} %copy-done, f32[2,1024]{1,0:T(2,128)S(1)} %copy-done.2, bf16[2,1024]{1,0:T(2,128)(2,1)S(1)} %copy-done.3, f32[4,128]{1,0:T(4,128)S(1)} %far_score.1.after_ref), custom_call_target="tpu_custom_call" | custom-call | flops 536870912 | bytes 1000000 | tf_op jit(solution)/shard_map/ensemble/pallas_call | solution.py:456
  28.9 2.1 %collective-permute-done.10 = f32[8,128]{1,0:T(8,128)S(1)} collective-permute-done((f32[8,128]{1,0:T(8,128)S(1)}, f32[8,128]{1,0:T(8,128)S(1)}, u32[]{:S(2)}, u32[]{:S(2)}) %collective-permute-start.10) | collective-permute-done | bytes 4128 | tf_op jit(solution)/shard_map/ppermute | solution.py:440
  31.1 0.4 %expand.1 = (bf16[96,1024]{1,0:T(8,128)(2,1)S(1)}, s32[1,1024]{1,0:T(1,128)S(1)}) custom-call(s32[256,3]{1,0:T(8,128)S(1)} %get-tuple-element.31.where_ref, f32[2,128]{1,0:T(2,128)S(1)} %ensemble.4.after_ref), custom_call_target="tpu_custom_call" | custom-call | flops 100000000 | bytes 1000000 | tf_op jit(solution)/shard_map/expand/pallas_call | solution.py:513
  31.5 0.7 %collective-permute-done.11.far_ref = f32[24,128]{1,0:T(8,128)S(1)} collective-permute-done((f32[24,128]{1,0:T(8,128)S(1)}, f32[24,128]{1,0:T(8,128)S(1)}, u32[]{:S(2)}, u32[]{:S(2)}) %collective-permute-start.11) | collective-permute-done | bytes 12320 | tf_op jit(solution)/shard_map/ppermute | solution.py:385
  32.3 0.9 %finish.1 = f32[1,1024]{1,0:T(1,128)} custom-call(bf16[96,1024]{1,0:T(8,128)(2,1)S(1)} %get-tuple-element.50.line_ref, s32[1,1024]{1,0:T(1,128)S(1)} %get-tuple-element.51.lane_ref, f32[24,128]{1,0:T(8,128)S(1)} %concatenate.8.near_ref, f32[24,128]{1,0:T(8,128)S(1)} %collective-permute-done.11.far_ref), custom_call_target="tpu_custom_call" | custom-call | flops 1000000 | bytes 1000000 | tf_op jit(solution)/shard_map/finish/pallas_call | solution.py:523
  (33 shorter events, 0.5 us)
Async XLA Ops:
  0.0 7.8 %collective-permute-start = (bf16[3,512,256]{2,1,0:T(8,128)(2,1)}, bf16[3,512,256]{2,1,0:T(8,128)(2,1)S(1)}, u32[]{:S(2)}, u32[]{:S(2)}) collective-permute-start(bf16[3,512,256]{2,1,0:T(8,128)(2,1)} %qkv_hbm.1), channel_id=1, source_target_pairs={{0,1},{1,0},{2,3},{3,2},{4,5},{5,4},{6,7},{7,6},{8,9},{9,8},{10,11... | collective-permute-start | bytes 2359304 | tf_op jit(solution)/shard_map/ppermute | solution.py:385
  0.5 7.4 %copy-start.4 = (f32[4,512]{1,0:T(4,128)S(1)}, f32[4,512]{1,0:T(4,128)}, u32[]{:S(2)}) copy-start(f32[4,512]{1,0:T(4,128)} %scale_ref.1) | copy-start | bytes 24580
  0.5 7.4 %copy-start.5 = (f32[4,512]{1,0:T(4,128)S(1)}, f32[4,512]{1,0:T(4,128)}, u32[]{:S(2)}) copy-start(f32[4,512]{1,0:T(4,128)} %shift_ref.1) | copy-start | bytes 24580
  0.5 7.4 %copy-start.6 = (f32[512]{0:T(512)S(1)}, f32[512]{0:T(512)}, u32[]{:S(2)}) copy-start(f32[512]{0:T(512)} %param.29) | copy-start | bytes 6148
  0.5 7.4 %copy-start.7 = (f32[512]{0:T(512)S(1)}, f32[512]{0:T(512)}, u32[]{:S(2)}) copy-start(f32[512]{0:T(512)} %param.30) | copy-start | bytes 6148
  0.5 7.4 %copy-start.8 = (f32[512]{0:T(512)S(1)}, f32[512]{0:T(512)}, u32[]{:S(2)}) copy-start(f32[512]{0:T(512)} %param.26) | copy-start | bytes 6148
  0.5 7.4 %copy-start.9 = (f32[512]{0:T(512)S(1)}, f32[512]{0:T(512)}, u32[]{:S(2)}) copy-start(f32[512]{0:T(512)} %param.33) | copy-start | bytes 6148
  4.5 4.4 %collective-permute-start.2 = (bf16[512,512]{1,0:T(8,128)(2,1)S(1)}, bf16[512,512]{1,0:T(8,128)(2,1)S(1)}, u32[]{:S(2)}, u32[]{:S(2)}) collective-permute-start(bf16[512,512]{1,0:T(8,128)(2,1)S(1)} %get-tuple-element.37.fw0_ref.refs_1_), channel_id=1, source_target_pairs={{0,1},{1,0},{2,3},{3,2},{4,5},{5,4},{6,7},{7,6},{8,9},{9,8},{10,11... | collective-permute-start | bytes 1572872 | tf_op jit(solution)/shard_map/ppermute | solution.py:385
  4.6 10.8 %collective-permute-start.6 = (bf16[528,512]{1,0:T(8,128)(2,1)S(1)}, bf16[528,512]{1,0:T(8,128)(2,1)S(1)}, u32[]{:S(2)}, u32[]{:S(2)}) collective-permute-start(bf16[528,512]{1,0:T(8,128)(2,1)S(1)} %get-tuple-element.42.refs_3_), channel_id=1, source_target_pairs={{0,1},{1,0},{2,3},{3,2},{4,5},{5,4},{6,7},{7,6},{8,9},{9,8},{10,11... | collective-permute-start | bytes 1622024 | tf_op jit(solution)/shard_map/ppermute | solution.py:385
  5.1 16.7 %collective-permute-start.8 = (bf16[528,512]{1,0:T(8,128)(2,1)S(1)}, bf16[528,512]{1,0:T(8,128)(2,1)S(1)}, u32[]{:S(2)}, u32[]{:S(2)}) collective-permute-start(bf16[528,512]{1,0:T(8,128)(2,1)S(1)} %get-tuple-element.42.refs_3_), channel_id=1, source_target_pairs={{0,2},{2,0},{4,6},{6,4},{8,10},{10,8},{12,14},{14,12},{1,3},{3,1},... | collective-permute-start | bytes 1622024 | tf_op jit(solution)/shard_map/ppermute | solution.py:414
  7.7 1.2 %collective-permute-start.1 = (bf16[128,128]{1,0:T(8,128)(2,1)S(1)}, bf16[128,128]{1,0:T(8,128)(2,1)S(1)}, u32[]{:S(2)}, u32[]{:S(2)}) collective-permute-start(bf16[128,128]{1,0:T(8,128)(2,1)S(1)} %get-tuple-element.34), channel_id=1, source_target_pairs={{0,1},{1,0},{2,3},{3,2},{4,5},{5,4},{6,7},{7,6},{8,9},{9,8},{10,11... | collective-permute-start | bytes 98312 | tf_op jit(solution)/shard_map/ppermute | solution.py:385
  8.6 6.8 %copy-start = (bf16[2,512,1024]{2,1,0:T(8,128)(2,1)S(1)}, bf16[2,512,1024]{2,1,0:T(8,128)(2,1)}, u32[]{:S(2)}) copy-start(bf16[2,512,1024]{2,1,0:T(8,128)(2,1)} %w_ref.5) | copy-start | bytes 6291460
  8.6 6.8 %copy-start.1 = (bf16[1024,512]{1,0:T(8,128)(2,1)S(1)}, bf16[1024,512]{1,0:T(8,128)(2,1)}, u32[]{:S(2)}) copy-start(bf16[1024,512]{1,0:T(8,128)(2,1)} %feat_ref.5) | copy-start | bytes 3145732
  8.6 6.8 %copy-start.2 = (f32[2,1024]{1,0:T(2,128)S(1)}, f32[2,1024]{1,0:T(2,128)}, u32[]{:S(2)}) copy-start(f32[2,1024]{1,0:T(2,128)} %bias_ref.5) | copy-start | bytes 24580
  8.7 6.8 %copy-start.3 = (bf16[2,1024]{1,0:T(2,128)(2,1)S(1)}, bf16[2,1024]{1,0:T(2,128)(2,1)}, u32[]{:S(2)}) copy-start(bf16[2,1024]{1,0:T(2,128)(2,1)} %out_ref.5) | copy-start | bytes 12292
  11.0 6.9 %collective-permute-start.3 = (bf16[64,512]{1,0:T(8,128)(2,1)S(1)}, bf16[64,512]{1,0:T(8,128)(2,1)S(1)}, u32[]{:S(2)}, u32[]{:S(2)}) collective-permute-start(bf16[64,512]{1,0:T(8,128)(2,1)S(1)} %get-tuple-element.38), channel_id=1, source_target_pairs={{0,12},{2,14},{4,8},{6,10},{8,4},{10,6},{12,0},{14,2},{1,13},{3,15... | collective-permute-start | bytes 196616 | tf_op jit(solution)/shard_map/ppermute | solution.py:440
  14.7 5.9 %collective-permute-start.4 = (bf16[64,512]{1,0:T(8,128)(2,1)S(1)}, bf16[64,512]{1,0:T(8,128)(2,1)S(1)}, u32[]{:S(2)}, u32[]{:S(2)}) collective-permute-start(bf16[64,512]{1,0:T(8,128)(2,1)S(1)} %get-tuple-element.39), channel_id=1, source_target_pairs={{0,8},{2,10},{4,12},{6,14},{8,0},{10,2},{12,4},{14,6},{1,9},{3,11}... | collective-permute-start | bytes 196616 | tf_op jit(solution)/shard_map/ppermute | solution.py:440
  14.7 5.9 %collective-permute-start.5 = (bf16[64,512]{1,0:T(8,128)(2,1)S(1)}, bf16[64,512]{1,0:T(8,128)(2,1)S(1)}, u32[]{:S(2)}, u32[]{:S(2)}) collective-permute-start(bf16[64,512]{1,0:T(8,128)(2,1)S(1)} %get-tuple-element.40), channel_id=1, source_target_pairs={{0,4},{2,6},{4,0},{6,2},{8,12},{10,14},{12,8},{14,10},{1,5},{3,7},... | collective-permute-start | bytes 196616 | tf_op jit(solution)/shard_map/ppermute | solution.py:440
  21.0 1.4 %collective-permute-start.7 = (bf16[128,512]{1,0:T(8,128)(2,1)S(1)}, bf16[128,512]{1,0:T(8,128)(2,1)S(1)}, u32[]{:S(2)}, u32[]{:S(2)}) collective-permute-start(bf16[128,512]{1,0:T(8,128)(2,1)S(1)} %get-tuple-element.49.mine_ref), channel_id=1, source_target_pairs={{0,1},{1,0},{2,3},{3,2},{4,5},{5,4},{6,7},{7,6},{8,9},{9,8},{10,11... | collective-permute-start | bytes 393224 | tf_op jit(solution)/shard_map/ppermute | solution.py:385
  22.8 3.7 %collective-permute-start.9 = (f32[4,128]{1,0:T(4,128)S(1)}, f32[4,128]{1,0:T(4,128)S(1)}, u32[]{:S(2)}, u32[]{:S(2)}) collective-permute-start(f32[4,128]{1,0:T(4,128)S(1)} %far_score.1.after_ref), channel_id=1, source_target_pairs={{0,4},{2,6},{4,0},{6,2},{8,12},{10,14},{12,8},{14,10},{1,5},{3,7},... | collective-permute-start | bytes 6152 | tf_op jit(solution)/shard_map/ppermute | solution.py:440
  26.5 4.5 %collective-permute-start.10 = (f32[8,128]{1,0:T(8,128)S(1)}, f32[8,128]{1,0:T(8,128)S(1)}, u32[]{:S(2)}, u32[]{:S(2)}) collective-permute-start(f32[8,128]{1,0:T(8,128)S(1)} %pad_maximum_fusion), channel_id=1, source_target_pairs={{0,8},{2,10},{4,12},{6,14},{8,0},{10,2},{12,4},{14,6},{1,9},{3,11}... | collective-permute-start | bytes 12296 | tf_op jit(solution)/shard_map/ppermute | solution.py:440
  31.0 1.2 %collective-permute-start.11 = (f32[24,128]{1,0:T(8,128)S(1)}, f32[24,128]{1,0:T(8,128)S(1)}, u32[]{:S(2)}, u32[]{:S(2)}) collective-permute-start(f32[24,128]{1,0:T(8,128)S(1)} %concatenate.8.near_ref), channel_id=1, source_target_pairs={{0,1},{1,0},{2,3},{3,2},{4,5},{5,4},{6,7},{7,6},{8,9},{9,8},{10,11... | collective-permute-start | bytes 36872 | tf_op jit(solution)/shard_map/ppermute | solution.py:385
